TPU v7x, 32 devices: a whole 2x2x4 slice. The times are simulated.
32 devices in a mesh: row: 4 (over y, x), col: 8 (over z, core).
Axes of the slice: x: 2, y: 2, z: 4, core: 2. Of those that a mesh axis runs over, the one named last changes fastest.
Arguments:
- factor: bfloat16 [4, 12, 512, 8, 1, 512], P('row', None, None, 'col'), may hold values from -0.03125 to 0.03125, as said below
- diag_inverse: float32 [4, 2, 1024, 512], P('row'), may hold values from -0.088388348 to 1.5, as said below
- residuals: float32 [256, 12, 4, 512], P('row', None, None, 'col'), may hold values from -6 to 6
Outputs:
- solved: float32 [256, 2, 4, 512], P('col', None, 'row')
- trailing: float32 [256, 10, 4, 512], P('col', None, 'row')
Inputs may be any that keep to these rules, and one draw needn't show every extreme that they name: factor is zero wherever its row block halved (rounded down) is not above its column block halved. `diag_inverse`: each pair's inverse, assembled from its two blocks' columns, is lower triangular with diagonal entries from 0.5 to 1.5.
All inputs are finite; a program needn't handle non-finite values.
Results may differ from a plain program's by a relative error of at most 0.0095.
Values may be sent and summed in bfloat16 or wider, within the bound.
A program may use at most 64 MiB of HBM per device.

v0:
```python
import jax
import jax.numpy as jnp
from jax import lax
from jax.sharding import PartitionSpec as P


def shards(factor, diag_inverse, residuals):
    row_count = lax.axis_size("row")
    col_count = lax.axis_size("col")
    my_row = lax.axis_index("row")
    my_col = lax.axis_index("col")
    local_factor = factor[0, :, :, 0]
    blocks_here = local_factor.shape[0]
    block_width = local_factor.shape[1]
    panel_count = local_factor.shape[2]
    flat_factor = local_factor.reshape(blocks_here, block_width, panel_count * block_width)
    inverses = diag_inverse[0]
    diag_blocks = inverses.shape[0]
    relaid = lax.all_to_all(
        lax.all_to_all(
            residuals.astype(jnp.bfloat16), "row", split_axis=2, concat_axis=0, tiled=True
        ),
        "col",
        split_axis=0,
        concat_axis=3,
        tiled=True,
    ).astype(residuals.dtype)
    own_rhs = relaid[:, :, 0, :]
    slice_width = own_rhs.shape[0]
    walker_total = slice_width * col_count
    pair_total = panel_count * col_count // 2
    known_start = jnp.zeros((walker_total, panel_count * block_width), jnp.bfloat16)
    solved_start = jnp.zeros((slice_width, diag_blocks, block_width), jnp.float32)
    walker_start = my_col * slice_width

    def one_pair(pair_index, loop_state):
        known_blocks, solved_local = loop_state
        first_block = (2 * jnp.asarray(pair_index)).astype(jnp.int32)
        local_block = first_block // row_count
        first_row = first_block % row_count
        is_second = my_row == first_row + 1
        owns = jnp.logical_or(my_row == first_row, is_second)
        block_factor = lax.dynamic_index_in_dim(flat_factor, local_block, 0, keepdims=False)
        partial_value = lax.dot_general(
            known_blocks, block_factor, (((1,), (1,)), ((), ())), preferred_element_type=jnp.float32
        )
        rounded = lax.optimization_barrier(partial_value.astype(jnp.bfloat16)).astype(jnp.float32)
        rhs_block = lax.dynamic_index_in_dim(own_rhs, local_block, 1, keepdims=False)
        inverse = lax.dynamic_index_in_dim(inverses, local_block, 0, keepdims=False)
        rhs_full = lax.dynamic_update_slice(
            jnp.zeros((walker_total, block_width), jnp.float32),
            rhs_block,
            (walker_start, jnp.int32(0)),
        )
        term = lax.dot_general(
            rhs_full - rounded,
            inverse,
            (((1,), (1,)), ((), ())),
            precision=lax.Precision.HIGHEST,
            preferred_element_type=jnp.float32,
        )
        term = jnp.where(owns, term, 0.0)
        pair_solution = lax.psum(term, ("row", "col"))
        own_part = lax.dynamic_slice_in_dim(pair_solution, walker_start, slice_width, 0)
        pair_rounded = pair_solution.astype(jnp.bfloat16)
        own_block = jnp.where(is_second, own_part[:, block_width:], own_part[:, :block_width])
        updated = lax.dynamic_update_index_in_dim(solved_local, own_block, local_block, 1)
        solved_local = jnp.where(owns, updated, solved_local)
        for half in range(2):
            block_index = first_block + half
            placed = pair_rounded[:, half * block_width : (half + 1) * block_width]
            known_blocks = jnp.where(my_col == block_index % col_count, placed, known_blocks)
        return (known_blocks, solved_local)

    known_blocks, solved_local = lax.fori_loop(0, pair_total, one_pair, (known_start, solved_start))
    trail_factor = flat_factor[diag_blocks:]
    trail_summed = lax.psum_scatter(
        lax.dot_general(
            known_blocks, trail_factor, (((1,), (2,)), ((), ())), preferred_element_type=jnp.float32
        ).astype(jnp.bfloat16),
        "col",
        scatter_dimension=0,
        tiled=True,
    ).astype(jnp.float32)
    trailing = own_rhs[:, diag_blocks:, :] - trail_summed
    return (solved_local[:, :, None, :], trailing[:, :, None, :])


def solution(mesh):
    placed = (
        P("row", None, None, "col", None, None),
        P("row", None, None, None),
        P("row", None, None, "col"),
    )
    return jax.shard_map(
        shards,
        mesh=mesh,
        in_specs=placed,
        out_specs=(P("col", None, "row", None), P("col", None, "row", None)),
        check_vma=False,
    )
```

profile of v0, /device:TPU:0, one launch (start us, length us, event | category | flops | bytes accessed | tf_op | source)
XLA Modules:
  0.0 657.8 jit_solution(17106109122414137565)
XLA Ops:
  8.0 1.9 copy.40
  11.1 12.1 %all_to_all.27 = bf16[4,2,24576]{2,1,0:T(2,128)(2,1)S(1)} all-to-all(bf16[4,2,24576]{2,1,0:T(2,128)(2,1)S(1)} %reshape.16), channel_id=1, replica_groups=mesh['row'=4,'col'=8] {'row'}, dimensions={0} | all-to-all | bytes 786432 | tf_op jit(solution)/shard_map/all_to_all | solution.py:20
  23.7 1.3 reshape.18
  25.1 4.9 all-to-all-start.1
  29.9 12.6 %all-to-all-done.1 = bf16[8,2,12288]{2,1,0:T(2,128)(2,1)S(1)} async-done(((bf16[8,2,12288]{2,1,0:T(2,128)(2,1)}), bf16[8,2,12288]{2,1,0:T(2,128)(2,1)S(1)}, u32[]{:S(2)}, u32[]{:S(2)}) %all-to-all-start.1) | async-done | bytes 393248 | tf_op jit(solution)/shard_map/all_to_all | solution.py:19
  43.5 1.1 copy.30
  45.0 560.8 %while.19 = (s32[]{:T(128)}, bf16[256,512]{1,0:T(8,128)(2,1)S(1)}, f32[32,2,512]{2,0,1:T(8,128)S(1)}, s32[]{:T(128)}, s32[]{:T(128)}, /*index=5*/f32[32,12,512]{...) while((s32[]{:T(128)}, bf16[256,512]{1,0:T(8,128)(2,1)S(1)}, ...), condition=%wide.region_2.3_spmd.clone, body=%wide.region_0.2_spmd.clone.sunk | while | flops 1746567168 | bytes 15074070 | solution.py:75
  45.3 1.4 fusion.33
  46.7 1.9 dynamic_update_slice.17
  48.6 6.1 fusion.34
  54.8 126.8 %all-reduce.2.cloned.1.call-done = f32[256,1024]{1,0:T(8,128)} async-done(((f32[256,1024]{1,0:T(8,128)}), f32[256,1024]{1,0:T(8,128)}) %all-reduce.2.cloned.1.call-update) | async-done | bytes 1048592 | tf_op jit(solution)/shard_map/while/body/eval_jaxpr/psum | solution.py:63
  181.7 1.3 convert_element_type.89
  183.1 0.9 fusion.36
  184.3 1.4 fusion.33
  185.7 1.9 dynamic_update_slice.17
  187.7 6.1 fusion.34
  193.9 128.4 %all-reduce.2.cloned.1.call-done = f32[256,1024]{1,0:T(8,128)} async-done(((f32[256,1024]{1,0:T(8,128)}), f32[256,1024]{1,0:T(8,128)}) %all-reduce.2.cloned.1.call-update) | async-done | bytes 1048592 | tf_op jit(solution)/shard_map/while/body/eval_jaxpr/psum | solution.py:63
  322.3 1.3 convert_element_type.89
  324.9 1.4 fusion.33
  326.3 1.9 dynamic_update_slice.17
  328.3 6.1 fusion.34
  334.5 128.4 %all-reduce.2.cloned.1.call-done = f32[256,1024]{1,0:T(8,128)} async-done(((f32[256,1024]{1,0:T(8,128)}), f32[256,1024]{1,0:T(8,128)}) %all-reduce.2.cloned.1.call-update) | async-done | bytes 1048592 | tf_op jit(solution)/shard_map/while/body/eval_jaxpr/psum | solution.py:63
  462.9 1.3 convert_element_type.89
  465.5 1.4 fusion.33
  467.0 1.9 dynamic_update_slice.17
  468.9 6.1 fusion.34
  475.1 128.4 %all-reduce.2.cloned.1.call-done = f32[256,1024]{1,0:T(8,128)} async-done(((f32[256,1024]{1,0:T(8,128)}), f32[256,1024]{1,0:T(8,128)}) %all-reduce.2.cloned.1.call-update) | async-done | bytes 1048592 | tf_op jit(solution)/shard_map/while/body/eval_jaxpr/psum | solution.py:63
  603.5 1.3 convert_element_type.89
  605.9 5.6 fusion.20
  612.3 35.8 %reduce-scatter.2.cloned.1.call-done = bf16[32,10,512]{2,0,1:T(8,128)(2,1)} async-done(((bf16[256,10,512]{2,0,1:T(8,128)(2,1)}), bf16[32,10,512]{2,0,1:T(8,128)(2,1)}) %reduce-scatter.2.cloned.1.call-update) | async-done | bytes 327696 | tf_op jit(solution)/shard_map/reduce_scatter | solution.py:77
  648.1 1.1 fusion.21
  649.2 1.5 copy.34
  (39 shorter events, 8.1 us)
Async XLA Ops:
  25.1 17.4 %all-to-all-start.1 = ((bf16[8,2,12288]{2,1,0:T(2,128)(2,1)}), bf16[8,2,12288]{2,1,0:T(2,128)(2,1)S(1)}, u32[]{:S(2)}, u32[]{:S(2)}) async-start(bf16[8,2,12288]{2,1,0:T(2,128)(2,1)} %reshape.18), calls=%async_computation.1 | async-start | bytes 786432 | tf_op jit(solution)/shard_map/all_to_all | solution.py:19
  45.0 136.6 %all-reduce.2.cloned.1.call-start = ((), (), s32[]{:S(2)}) async-start(), calls=%async_computation.4 | async-start | bytes 2097152 | tf_op jit(solution)/shard_map/while/body/eval_jaxpr/psum | solution.py:63
  184.0 138.2 %all-reduce.2.cloned.1.call-start = ((), (), s32[]{:S(2)}) async-start(), calls=%async_computation.4 | async-start | bytes 2097152 | tf_op jit(solution)/shard_map/while/body/eval_jaxpr/psum | solution.py:63
  324.7 138.2 %all-reduce.2.cloned.1.call-start = ((), (), s32[]{:S(2)}) async-start(), calls=%async_computation.4 | async-start | bytes 2097152 | tf_op jit(solution)/shard_map/while/body/eval_jaxpr/psum | solution.py:63
  465.3 138.2 %all-reduce.2.cloned.1.call-start = ((), (), s32[]{:S(2)}) async-start(), calls=%async_computation.4 | async-start | bytes 2097152 | tf_op jit(solution)/shard_map/while/body/eval_jaxpr/psum | solution.py:63
  605.9 42.2 %reduce-scatter.2.cloned.1.call-start = ((), (), s32[]{:S(2)}) async-start(), calls=%async_computation.3 | async-start | bytes 2949120 | tf_op jit(solution)/shard_map/reduce_scatter | solution.py:77
Sparse Core Ops, SparseCore 0:
  54.9 126.7 all-reduce.1
  193.9 128.3 all-reduce.1
  334.5 128.3 all-reduce.1
  475.1 128.3 all-reduce.1
Sparse Core Ops, SparseCore 1:
  611.6 36.5 reduce-scatter.1
where the time goes:
time: 659 us; the launch traced here: 658 us
  waiting for transfers between devices  561 us (85%)
  matrix products  35.5 us (5%)
  local copies, waits for them, and re-layouts  17.9 us (3%)
  between operations  15.2 us (2%)
  blocking collectives  12.1 us (2%)
  other arithmetic  10.6 us (2%)
    psum x4, waiting for transfers between devices, one_pair(): pair_solution = lax.psum(term, ('row', 'col'))  512 us
    reduce_scatter x1, waiting for transfers between devices, shards(): lax.psum_scatter(lax.dot_general(known_blocks, trail_factor, (((1,), (2,)...  35.8 us
    dot_general x4, matrix products, one_pair(): lax.dot_general(rhs_full - rounded, inverse, (((1,), (1,)), ((), ())), pr...  24.5 us
  transfers between devices with their start and end apart: 6, of which 6 were waited for; matrix products, arithmetic and copies ran while one was open for 0% of the time, Pallas kernels for 0%

commit v1 on v0

--- a/solution.py
+++ b/solution.py
@@ -60,7 +60,9 @@
             preferred_element_type=jnp.float32,
         )
         term = jnp.where(owns, term, 0.0)
-        pair_solution = lax.psum(term, ("row", "col"))
+        pair_solution = term
+        for name in ("col", "row"):
+            pair_solution = lax.psum(pair_solution, name)
         own_part = lax.dynamic_slice_in_dim(pair_solution, walker_start, slice_width, 0)
         pair_rounded = pair_solution.astype(jnp.bfloat16)
         own_block = jnp.where(is_second, own_part[:, block_width:], own_part[:, :block_width])

time: 659 us -> 597 us (0.906)
  waiting for transfers between devices: 561 us -> 499 us
    psum x4 -> x8, waiting for transfers between devices: 512 us -> 449 us  [one_pair(): pair_solution = lax.psum(pair_solution, name)]
  transfers between devices with their start and end apart: 6 -> 10, of which waited for: 6 -> 10; matrix products, arithmetic and copies ran while one was open for 0% -> 0% of each run, Pallas kernels for 0% -> 0%
where the time goes in v1:
time: 597 us; the launch traced here: 596 us
  waiting for transfers between devices  499 us (84%)
  matrix products  35.6 us (6%)
  local copies, waits for them, and re-layouts  17.9 us (3%)
  between operations  15.5 us (3%)
  blocking collectives  12.1 us (2%)
  other arithmetic  10.6 us (2%)
    psum x8, waiting for transfers between devices, one_pair(): pair_solution = lax.psum(pair_solution, name)  449 us
    reduce_scatter x1, waiting for transfers between devices, shards(): lax.psum_scatter(lax.dot_general(known_blocks, trail_factor, (((1,), (2,)...  36.8 us
    dot_general x4, matrix products, one_pair(): lax.dot_general(rhs_full - rounded, inverse, (((1,), (1,)), ((), ())), pr...  24.5 us
    all_to_all x1, waiting for transfers between devices, shards(): lax.all_to_all(lax.all_to_all(residuals.astype(jnp.bfloat16), 'row', spli...  12.6 us
    all_to_all x1, blocking collectives, shards(): lax.all_to_all(residuals.astype(jnp.bfloat16), 'row', split_axis=2, conca...  12.1 us
  transfers between devices with their start and end apart: 10, of which 10 were waited for; matrix products, arithmetic and copies ran while one was open for 0% of the time, Pallas kernels for 0%

profile of v1, /device:TPU:0, one launch (start us, length us, event | category | flops | bytes accessed | tf_op | source)
XLA Modules:
  0.0 596.3 jit_solution(16061215601669823134)
XLA Ops:
  8.0 1.9 copy.40
  11.1 12.1 %all_to_all.27 = bf16[4,2,24576]{2,1,0:T(2,128)(2,1)S(1)} all-to-all(bf16[4,2,24576]{2,1,0:T(2,128)(2,1)S(1)} %reshape.16), channel_id=1, replica_groups=mesh['row'=4,'col'=8] {'row'}, dimensions={0} | all-to-all | bytes 786432 | tf_op jit(solution)/shard_map/all_to_all | solution.py:20
  23.7 1.3 reshape.18
  25.1 4.9 all-to-all-start.1
  29.9 12.6 %all-to-all-done.1 = bf16[8,2,12288]{2,1,0:T(2,128)(2,1)S(1)} async-done(((bf16[8,2,12288]{2,1,0:T(2,128)(2,1)}), bf16[8,2,12288]{2,1,0:T(2,128)(2,1)S(1)}, u32[]{:S(2)}, u32[]{:S(2)}) %all-to-all-start.1) | async-done | bytes 393248 | tf_op jit(solution)/shard_map/all_to_all | solution.py:19
  45.0 498.0 %while.19 = (s32[]{:T(128)}, bf16[256,512]{1,0:T(8,128)(2,1)S(1)}, f32[32,2,512]{2,0,1:T(8,128)S(1)}, s32[]{:T(128)}, s32[]{:T(128)}, /*index=5*/f32[32,12,512]{...) while((s32[]{:T(128)}, bf16[256,512]{1,0:T(8,128)(2,1)S(1)}, ...), condition=%wide.region_3.4_spmd.clone, body=%wide.region_0.3_spmd.clone.sunk | while | flops 1746829312 | bytes 21365560 | solution.py:77
  45.3 1.4 fusion.33
  46.7 1.9 dynamic_update_slice.17
  48.7 6.1 %fusion.34 = f32[256,1024]{1,0:T(8,128)} fusion(f32[2,1024,512]{2,1,0:T(8,128)} %get-tuple-element.466, s32[]{:T(128)S(6)} %select_n.283, f32[256,512]{0,1:T(8,128)S(1)} %dynamic_update_slice.17, bf16[256,512]{0,1:T(8,128)(2,1)S(1)} %fusion.33, pred[]{:T(512)S(6)} %or.13), kind=kOutput, calls=%fused_computation.3.clone.1 | convolution fusion | flops 1611137024 | bytes 3932165 | tf_op jit(solution)/shard_map/while/body/eval_jaxpr/dot_general | solution.py:55
  54.8 55.8 %all-reduce.3.cloned.1.call-done = f32[256,1024]{1,0:T(8,128)} async-done(((f32[256,1024]{1,0:T(8,128)}), f32[256,1024]{1,0:T(8,128)}) %all-reduce.3.cloned.1.call-update) | async-done | bytes 1048592 | tf_op jit(solution)/shard_map/while/body/eval_jaxpr/psum | solution.py:65
  110.7 54.5 %all-reduce.5.cloned.1.call-done = f32[256,1024]{1,0:T(8,128)} async-done(((f32[256,1024]{1,0:T(8,128)}), f32[256,1024]{1,0:T(8,128)}) %all-reduce.5.cloned.1.call-update) | async-done | bytes 1048592 | tf_op jit(solution)/shard_map/while/body/eval_jaxpr/psum | solution.py:65
  165.3 1.3 convert_element_type.89
  167.9 1.4 fusion.33
  169.3 1.9 dynamic_update_slice.17
  171.2 6.1 %fusion.34 = f32[256,1024]{1,0:T(8,128)} fusion(f32[2,1024,512]{2,1,0:T(8,128)} %get-tuple-element.466, s32[]{:T(128)S(6)} %select_n.283, f32[256,512]{0,1:T(8,128)S(1)} %dynamic_update_slice.17, bf16[256,512]{0,1:T(8,128)(2,1)S(1)} %fusion.33, pred[]{:T(512)S(6)} %or.13), kind=kOutput, calls=%fused_computation.3.clone.1 | convolution fusion | flops 1611137024 | bytes 3932165 | tf_op jit(solution)/shard_map/while/body/eval_jaxpr/dot_general | solution.py:55
  177.4 58.5 %all-reduce.3.cloned.1.call-done = f32[256,1024]{1,0:T(8,128)} async-done(((f32[256,1024]{1,0:T(8,128)}), f32[256,1024]{1,0:T(8,128)}) %all-reduce.3.cloned.1.call-update) | async-done | bytes 1048592 | tf_op jit(solution)/shard_map/while/body/eval_jaxpr/psum | solution.py:65
  236.0 54.4 %all-reduce.5.cloned.1.call-done = f32[256,1024]{1,0:T(8,128)} async-done(((f32[256,1024]{1,0:T(8,128)}), f32[256,1024]{1,0:T(8,128)}) %all-reduce.5.cloned.1.call-update) | async-done | bytes 1048592 | tf_op jit(solution)/shard_map/while/body/eval_jaxpr/psum | solution.py:65
  290.4 1.3 convert_element_type.89
  293.0 1.4 fusion.33
  294.4 1.9 dynamic_update_slice.17
  296.3 6.1 %fusion.34 = f32[256,1024]{1,0:T(8,128)} fusion(f32[2,1024,512]{2,1,0:T(8,128)} %get-tuple-element.466, s32[]{:T(128)S(6)} %select_n.283, f32[256,512]{0,1:T(8,128)S(1)} %dynamic_update_slice.17, bf16[256,512]{0,1:T(8,128)(2,1)S(1)} %fusion.33, pred[]{:T(512)S(6)} %or.13), kind=kOutput, calls=%fused_computation.3.clone.1 | convolution fusion | flops 1611137024 | bytes 3932165 | tf_op jit(solution)/shard_map/while/body/eval_jaxpr/dot_general | solution.py:55
  302.5 58.4 %all-reduce.3.cloned.1.call-done = f32[256,1024]{1,0:T(8,128)} async-done(((f32[256,1024]{1,0:T(8,128)}), f32[256,1024]{1,0:T(8,128)}) %all-reduce.3.cloned.1.call-update) | async-done | bytes 1048592 | tf_op jit(solution)/shard_map/while/body/eval_jaxpr/psum | solution.py:65
  361.0 54.4 %all-reduce.5.cloned.1.call-done = f32[256,1024]{1,0:T(8,128)} async-done(((f32[256,1024]{1,0:T(8,128)}), f32[256,1024]{1,0:T(8,128)}) %all-reduce.5.cloned.1.call-update) | async-done | bytes 1048592 | tf_op jit(solution)/shard_map/while/body/eval_jaxpr/psum | solution.py:65
  418.0 1.4 fusion.33
  419.5 1.9 dynamic_update_slice.17
  421.4 6.1 %fusion.34 = f32[256,1024]{1,0:T(8,128)} fusion(f32[2,1024,512]{2,1,0:T(8,128)} %get-tuple-element.466, s32[]{:T(128)S(6)} %select_n.283, f32[256,512]{0,1:T(8,128)S(1)} %dynamic_update_slice.17, bf16[256,512]{0,1:T(8,128)(2,1)S(1)} %fusion.33, pred[]{:T(512)S(6)} %or.13), kind=kOutput, calls=%fused_computation.3.clone.1 | convolution fusion | flops 1611137024 | bytes 3932165 | tf_op jit(solution)/shard_map/while/body/eval_jaxpr/dot_general | solution.py:55
  427.6 58.5 %all-reduce.3.cloned.1.call-done = f32[256,1024]{1,0:T(8,128)} async-done(((f32[256,1024]{1,0:T(8,128)}), f32[256,1024]{1,0:T(8,128)}) %all-reduce.3.cloned.1.call-update) | async-done | bytes 1048592 | tf_op jit(solution)/shard_map/while/body/eval_jaxpr/psum | solution.py:65
  486.2 54.5 %all-reduce.5.cloned.1.call-done = f32[256,1024]{1,0:T(8,128)} async-done(((f32[256,1024]{1,0:T(8,128)}), f32[256,1024]{1,0:T(8,128)}) %all-reduce.5.cloned.1.call-update) | async-done | bytes 1048592 | tf_op jit(solution)/shard_map/while/body/eval_jaxpr/psum | solution.py:65
  540.7 1.3 convert_element_type.89
  543.1 5.6 fusion.20
  549.5 36.8 %reduce-scatter.2.cloned.1.call-done = bf16[32,10,512]{2,0,1:T(8,128)(2,1)} async-done(((bf16[256,10,512]{2,0,1:T(8,128)(2,1)}), bf16[32,10,512]{2,0,1:T(8,128)(2,1)}) %reduce-scatter.2.cloned.1.call-update) | async-done | bytes 327696 | tf_op jit(solution)/shard_map/reduce_scatter | solution.py:79
  587.3 1.5 copy.34
  (51 shorter events, 12.7 us)
Async XLA Ops:
  25.1 17.4 %all-to-all-start.1 = ((bf16[8,2,12288]{2,1,0:T(2,128)(2,1)}), bf16[8,2,12288]{2,1,0:T(2,128)(2,1)S(1)}, u32[]{:S(2)}, u32[]{:S(2)}) async-start(bf16[8,2,12288]{2,1,0:T(2,128)(2,1)} %reshape.18), calls=%async_computation.1 | async-start | bytes 786432 | tf_op jit(solution)/shard_map/all_to_all | solution.py:19
  45.0 65.6 %all-reduce.3.cloned.1.call-start = ((), (), s32[]{:S(2)}) async-start(), calls=%async_computation.4 | async-start | bytes 2097152 | tf_op jit(solution)/shard_map/while/body/eval_jaxpr/psum | solution.py:65
  54.8 110.5 %all-reduce.5.cloned.1.call-start = ((), (), s32[]{:S(2)}) async-start(), calls=%async_computation.5 | async-start | bytes 2097152 | tf_op jit(solution)/shard_map/while/body/eval_jaxpr/psum | solution.py:65
  167.6 68.3 %all-reduce.3.cloned.1.call-start = ((), (), s32[]{:S(2)}) async-start(), calls=%async_computation.4 | async-start | bytes 2097152 | tf_op jit(solution)/shard_map/while/body/eval_jaxpr/psum | solution.py:65
  177.4 113.0 %all-reduce.5.cloned.1.call-start = ((), (), s32[]{:S(2)}) async-start(), calls=%async_computation.5 | async-start | bytes 2097152 | tf_op jit(solution)/shard_map/while/body/eval_jaxpr/psum | solution.py:65
  292.7 68.2 %all-reduce.3.cloned.1.call-start = ((), (), s32[]{:S(2)}) async-start(), calls=%async_computation.4 | async-start | bytes 2097152 | tf_op jit(solution)/shard_map/while/body/eval_jaxpr/psum | solution.py:65
  302.5 112.9 %all-reduce.5.cloned.1.call-start = ((), (), s32[]{:S(2)}) async-start(), calls=%async_computation.5 | async-start | bytes 2097152 | tf_op jit(solution)/shard_map/while/body/eval_jaxpr/psum | solution.py:65
  417.8 68.3 %all-reduce.3.cloned.1.call-start = ((), (), s32[]{:S(2)}) async-start(), calls=%async_computation.4 | async-start | bytes 2097152 | tf_op jit(solution)/shard_map/while/body/eval_jaxpr/psum | solution.py:65
  427.6 113.2 %all-reduce.5.cloned.1.call-start = ((), (), s32[]{:S(2)}) async-start(), calls=%async_computation.5 | async-start | bytes 2097152 | tf_op jit(solution)/shard_map/while/body/eval_jaxpr/psum | solution.py:65
  543.1 43.2 %reduce-scatter.2.cloned.1.call-start = ((), (), s32[]{:S(2)}) async-start(), calls=%async_computation.3 | async-start | bytes 2949120 | tf_op jit(solution)/shard_map/reduce_scatter | solution.py:79
Sparse Core Ops, SparseCore 0:
  54.9 55.7 all-reduce.2
  113.7 51.4 all-reduce.4
  177.5 58.3 all-reduce.2
  238.8 51.4 all-reduce.4
  302.6 58.3 all-reduce.2
  363.9 51.4 all-reduce.4
  427.7 58.3 all-reduce.2
  489.2 51.4 all-reduce.4
Sparse Core Ops, SparseCore 1:
  548.8 37.4 reduce-scatter.1
